TPU v7x, 32 devices: a whole 2x2x4 slice. The times are simulated.
32 devices in a mesh: row: 8 (over z, core), col: 2 (over x), depth: 2 (over y).
Axes of the slice: x: 2, y: 2, z: 4, core: 2. Of those that a mesh axis runs over, the one named last changes fastest.
Arguments:
- inputs: bfloat16 [1024, 6144], P(('depth', 'col'), 'row'), may hold values from -6 to 6
- cotangent: bfloat16 [1024, 6144], P(('depth', 'col'), 'row'), may hold values from -1.5 to 1.5
- w_in: bfloat16 [6144, 24576], P('row', 'col'), may hold values from -0.078125 to 0.078125
- w_out: bfloat16 [24576, 6144], P('col', 'row'), may hold values from -0.0390625 to 0.0390625
Outputs:
- outputs: bfloat16 [1024, 6144], P(('depth', 'col'), 'row')
- grad_inputs: bfloat16 [1024, 6144], P(('depth', 'col'), 'row')
- grad_w_in: bfloat16 [6144, 24576], P('row', ('col', 'depth'))
- grad_w_out: bfloat16 [24576, 6144], P('col', ('row', 'depth'))
All inputs are finite; a program needn't handle non-finite values.
Results may differ from a plain program's by a relative error of at most 0.03.
Values may be sent and summed in bfloat16 or wider, within the bound.
A program may use at most 192 MiB of HBM per device.

v0:
```python
import jax
import jax.numpy as jnp
from jax import lax
from jax.sharding import PartitionSpec as P

gelu_c = 0.7978845608028654
gelu_k = 0.044715


def gelu_pair(preact):
    inner = gelu_c * (preact + gelu_k * preact * preact * preact)
    tangent = jnp.tanh(inner)
    gelu_value = 0.5 * preact * (1.0 + tangent)
    gelu_slope = 0.5 * (1.0 + tangent) + 0.5 * preact * (1.0 - tangent * tangent) * gelu_c * (
        1.0 + 3.0 * gelu_k * preact * preact
    )
    return (gelu_value, gelu_slope)


def on_device(inputs, cotangent, w_in, w_out):
    x_all, dy_all = (
        lax.all_gather(inputs, "col", axis=0, tiled=True),
        lax.all_gather(cotangent, "col", axis=0, tiled=True),
    )
    preact = lax.psum_scatter(
        jnp.dot(x_all, w_in, preferred_element_type=jnp.float32).astype(jnp.bfloat16),
        "row",
        scatter_dimension=0,
        tiled=True,
    ).astype(jnp.float32)
    gelu_value, gelu_slope = gelu_pair(preact)
    hidden_all = lax.all_gather(gelu_value.astype(jnp.bfloat16), "row", axis=0, tiled=True)
    grad_hidden = lax.psum_scatter(
        lax.dot_general(
            dy_all, w_out, (((1,), (1,)), ((), ())), preferred_element_type=jnp.float32
        ).astype(jnp.bfloat16),
        "row",
        scatter_dimension=0,
        tiled=True,
    )
    grad_pre = (grad_hidden.astype(jnp.float32) * gelu_slope).astype(jnp.bfloat16)
    grad_pre_all = lax.all_gather(grad_pre, "row", axis=0, tiled=True)
    outputs = lax.psum_scatter(
        jnp.dot(hidden_all, w_out, preferred_element_type=jnp.float32).astype(jnp.bfloat16),
        "col",
        scatter_dimension=0,
        tiled=True,
    )
    grad_w_out_part = lax.dot_general(
        hidden_all, dy_all, (((0,), (0,)), ((), ())), preferred_element_type=jnp.float32
    )
    grad_inputs = lax.psum_scatter(
        lax.dot_general(
            grad_pre_all, w_in, (((1,), (1,)), ((), ())), preferred_element_type=jnp.float32
        ).astype(jnp.bfloat16),
        "col",
        scatter_dimension=0,
        tiled=True,
    )
    grad_w_in_part = lax.dot_general(
        x_all, grad_pre_all, (((0,), (0,)), ((), ())), preferred_element_type=jnp.float32
    )
    grad_w_in, grad_w_out = (
        lax.psum_scatter(
            grad_w_in_part.astype(jnp.bfloat16), "depth", scatter_dimension=1, tiled=True
        ).astype(jnp.float32),
        lax.psum_scatter(
            grad_w_out_part.astype(jnp.bfloat16), "depth", scatter_dimension=1, tiled=True
        ).astype(jnp.float32),
    )
    return (outputs, grad_inputs, grad_w_in.astype(jnp.bfloat16), grad_w_out.astype(jnp.bfloat16))


def solution(mesh):
    in_specs = (
        P(("depth", "col"), "row"),
        P(("depth", "col"), "row"),
        P("row", "col"),
        P("col", "row"),
    )
    out_specs = (
        P(("depth", "col"), "row"),
        P(("depth", "col"), "row"),
        P("row", ("col", "depth")),
        P("col", ("row", "depth")),
    )
    return jax.shard_map(
        on_device, mesh=mesh, in_specs=in_specs, out_specs=out_specs, check_vma=False
    )
```

profile of v0, /device:TPU:0, one launch (start us, length us, event | category | flops | bytes accessed | tf_op | source)
XLA Modules:
  0.0 1010.9 jit_solution(10807848610469497222)
XLA Ops:
  7.2 13.0 %all_gather.14 = bf16[512,768]{1,0:T(8,128)(2,1)S(1)} all-gather(bf16[256,768]{1,0:T(8,128)(2,1)} %param.5), channel_id=1, replica_groups=mesh['row'=8,'col'=2,'depth'=2] {'col'}, dimensions={0}, use_global_device_ids=true | all-gather | bytes 1179648 | tf_op jit(solution)/shard_map/all_gather | solution.py:23
  20.2 19.2 %convolution_convert_fusion.2 = bf16[512,12288]{1,0:T(8,128)(2,1)} fusion(bf16[512,768]{1,0:T(8,128)(2,1)S(1)} %all_gather.14, bf16[12288,768]{1,0:T(8,128)(2,1)} %param.7), kind=kOutput, calls=%fused_computation.3 | convolution fusion | flops 9669967872 | bytes 32243712 | tf_op jit(solution)/shard_map/dot_general | solution.py:34
  39.5 0.9 copy-done
  40.4 11.0 %all_gather.12 = bf16[512,768]{1,0:T(8,128)(2,1)S(1)} all-gather(bf16[256,768]{1,0:T(8,128)(2,1)S(1)} %copy-done), channel_id=1, replica_groups=mesh['row'=8,'col'=2,'depth'=2] {'col'}, dimensions={0}, use_global_device_ids=true | all-gather | bytes 1179648 | tf_op jit(solution)/shard_map/all_gather | solution.py:22
  51.4 18.7 %convolution_convert_fusion.3 = bf16[512,12288]{1,0:T(8,128)(2,1)} fusion(bf16[512,768]{1,0:T(8,128)(2,1)S(1)} %all_gather.12, bf16[768,12288]{1,0:T(8,128)(2,1)} %param.6), kind=kOutput, calls=%fused_computation.4 | convolution fusion | flops 9669967872 | bytes 32243712 | tf_op jit(solution)/shard_map/dot_general | solution.py:26
  70.2 100.1 %reduce-scatter.13.cloned.1.call-done = bf16[64,12288]{1,0:T(8,128)(2,1)} async-done(((bf16[512,12288]{1,0:T(8,128)(2,1)}), bf16[64,12288]{1,0:T(8,128)(2,1)}) %reduce-scatter.13.cloned.1.call-update) | async-done | bytes 1572880 | tf_op jit(solution)/shard_map/reduce_scatter | solution.py:33
  170.3 129.9 %reduce-scatter.9.cloned.1.call-done = bf16[64,12288]{1,0:T(8,128)(2,1)} async-done(((bf16[512,12288]{1,0:T(8,128)(2,1)}), bf16[64,12288]{1,0:T(8,128)(2,1)}) %reduce-scatter.9.cloned.1.call-update) | async-done | bytes 1572880 | tf_op jit(solution)/shard_map/reduce_scatter | solution.py:25
  300.2 4.9 fusion.8
  305.2 0.5 all-gather.5.cloned.1.call-update
  305.7 114.6 %all-gather.3.cloned.1.call-done = bf16[512,12288]{1,0:T(8,128)(2,1)} async-done(((bf16[64,12288]{1,0:T(8,128)(2,1)}), bf16[512,12288]{1,0:T(8,128)(2,1)}) %all-gather.3.cloned.1.call-update) | async-done | bytes 12582928 | tf_op jit(solution)/shard_map/all_gather | solution.py:32
  420.4 17.9 %convolution_convert_fusion = bf16[12288,768]{1,0:T(8,128)(2,1)} fusion(bf16[512,12288]{1,0:T(8,128)(2,1)} %all-gather.3.cloned.1.call-done, bf16[512,768]{1,0:T(8,128)(2,1)S(1)} %all_gather.14), kind=kOutput, calls=%fused_computation | convolution fusion | flops 9673113600 | bytes 32243712 | tf_op jit(solution)/shard_map/dot_general | solution.py:49
  438.3 24.8 %copy.10 = bf16[12288,768]{0,1:T(8,128)(2,1)} copy(bf16[12288,768]{1,0:T(8,128)(2,1)} %convolution_convert_fusion) | data formatting | bytes 37748736
  463.1 0.2 reduce-scatter.17.cloned.1.call-start
  463.3 74.1 %all-gather.5.cloned.1.call-done = bf16[512,12288]{1,0:T(8,128)(2,1)} async-done(((bf16[64,12288]{1,0:T(8,128)(2,1)}), bf16[512,12288]{1,0:T(8,128)(2,1)}) %all-gather.5.cloned.1.call-update) | async-done | bytes 12582928 | tf_op jit(solution)/shard_map/all_gather | solution.py:42
  537.4 17.9 %fusion = bf16[768,12288]{0,1:T(8,128)(2,1)} fusion(bf16[512,12288]{1,0:T(8,128)(2,1)} %all-gather.5.cloned.1.call-done, bf16[512,768]{1,0:T(8,128)(2,1)S(1)} %all_gather.12), kind=kOutput, calls=%fused_computation.2 | convolution fusion | flops 9673113600 | bytes 32243712 | tf_op jit(solution)/shard_map/dot_general | solution.py:60
  555.4 16.8 %convolution_convert_fusion.5 = bf16[512,768]{1,0:T(8,128)(2,1)} fusion(bf16[512,12288]{1,0:T(8,128)(2,1)} %all-gather.3.cloned.1.call-done, bf16[12288,768]{1,0:T(8,128)(2,1)} %param.7), kind=kOutput, calls=%fused_computation.24 | convolution fusion | flops 9664069632 | bytes 32243712 | tf_op jit(solution)/shard_map/dot_general | solution.py:44
  572.2 0.3 reduce-scatter.15.cloned.1.call-start
  572.5 16.7 %convolution_convert_fusion.4 = bf16[512,768]{1,0:T(8,128)(2,1)} fusion(bf16[512,12288]{1,0:T(8,128)(2,1)} %all-gather.5.cloned.1.call-done, bf16[768,12288]{1,0:T(8,128)(2,1)} %param.6), kind=kOutput, calls=%fused_computation.23 | convolution fusion | flops 9664069632 | bytes 32243712 | tf_op jit(solution)/shard_map/dot_general | solution.py:53
  589.2 160.3 %reduce-scatter.19.cloned.1.call-done = bf16[384,12288]{1,0:T(8,128)(2,1)} async-done(((bf16[768,12288]{1,0:T(8,128)(2,1)}), bf16[384,12288]{1,0:T(8,128)(2,1)}) %reduce-scatter.19.cloned.1.call-update) | async-done | bytes 9437200
  749.5 12.7 %copy.11 = bf16[12288,384]{1,0:T(8,128)(2,1)} copy(bf16[12288,384]{0,1:T(8,128)(2,1)} %bitcast.17) | data formatting | bytes 18874368
  762.2 201.2 %reduce-scatter.17.cloned.1.call-done = bf16[768,6144]{0,1:T(8,128)(2,1)} async-done(((bf16[768,12288]{0,1:T(8,128)(2,1)}), bf16[768,6144]{0,1:T(8,128)(2,1)}) %reduce-scatter.17.cloned.1.call-update) | async-done | bytes 9437200 | tf_op jit(solution)/shard_map/reduce_scatter | solution.py:64
  963.4 12.6 %copy.9 = bf16[768,6144]{1,0:T(8,128)(2,1)} copy(bf16[768,6144]{0,1:T(8,128)(2,1)} %reduce-scatter.17.cloned.1.call-done) | data formatting | bytes 18874368
  976.0 7.6 reduce-scatter.11.cloned.1.call-done
  983.6 20.4 %reduce-scatter.15.cloned.1.call-done = bf16[256,768]{1,0:T(8,128)(2,1)} async-done(((bf16[512,768]{1,0:T(8,128)(2,1)}), bf16[256,768]{1,0:T(8,128)(2,1)}) %reduce-scatter.15.cloned.1.call-update) | async-done | bytes 393232 | tf_op jit(solution)/shard_map/reduce_scatter | solution.py:52
  (14 shorter events, 0.4 us)
Async XLA Ops:
  7.2 163.1 %reduce-scatter.13.cloned.1.call-start = ((), (), s32[]{:S(2)}) async-start(), calls=%async_computation.9 | async-start | bytes 14155776 | tf_op jit(solution)/shard_map/reduce_scatter | solution.py:33
  39.4 1.0 copy-start
  39.5 260.8 %reduce-scatter.9.cloned.1.call-start = ((), (), s32[]{:S(2)}) async-start(), calls=%async_computation.6 | async-start | bytes 14155776 | tf_op jit(solution)/shard_map/reduce_scatter | solution.py:25
  70.1 350.2 %all-gather.3.cloned.1.call-start = ((), (), s32[]{:S(2)}) async-start(), calls=%async_computation.7 | async-start | bytes 14155776 | tf_op jit(solution)/shard_map/all_gather | solution.py:32
  305.1 232.3 %all-gather.5.cloned.1.call-start = ((), (), s32[]{:S(2)}) async-start(), calls=%async_computation.10 | async-start | bytes 14155776 | tf_op jit(solution)/shard_map/all_gather | solution.py:42
  305.7 443.8 %reduce-scatter.19.cloned.1.call-start = ((), (), s32[]{:S(2)}) async-start(), calls=%async_computation.13 | async-start | bytes 28311552
  463.1 500.3 %reduce-scatter.17.cloned.1.call-start = ((), (), s32[]{:S(2)}) async-start(), calls=%async_computation.12 | async-start | bytes 28311552 | tf_op jit(solution)/shard_map/reduce_scatter | solution.py:64
  555.4 428.3 %reduce-scatter.11.cloned.1.call-start = ((), (), s32[]{:S(2)}) async-start(), calls=%async_computation.8 | async-start | bytes 1179648 | tf_op jit(solution)/shard_map/reduce_scatter | solution.py:43
  572.2 431.8 %reduce-scatter.15.cloned.1.call-start = ((), (), s32[]{:S(2)}) async-start(), calls=%async_computation.11 | async-start | bytes 1179648 | tf_op jit(solution)/shard_map/reduce_scatter | solution.py:52
Sparse Core Ops, SparseCore 0:
  39.6 130.6 reduce-scatter.12
  172.6 127.5 reduce-scatter.8
  305.2 115.0 all-gather.2
  422.4 114.9 all-gather.4
  539.6 209.8 reduce-scatter.18
  751.7 211.6 reduce-scatter.16
  966.2 17.4 reduce-scatter.10
  986.6 17.4 reduce-scatter.14
where the time goes:
time: 1010 us
  waiting for transfers between devices  809 us (80%)
  matrix products  107 us (11%)
  local copies, waits for them, and re-layouts  51 us (5%)
  blocking collectives  23.9 us (2%)
  between operations  14.1 us (1%)
    reduce_scatter x1, waiting for transfers between devices, on_device(): lax.psum_scatter(grad_w_in_part.astype(jnp.bfloat16), 'depth', scatter_di...  201 us
    unnamed x9, waiting for transfers between devices  161 us
    reduce_scatter x1, waiting for transfers between devices, on_device(): lax.psum_scatter(jnp.dot(x_all, w_in, preferred_element_type=jnp.float32)...  130 us
    all_gather x1, waiting for transfers between devices, on_device(): lax.all_gather(gelu_value.astype(jnp.bfloat16), 'row', axis=0, tiled=True)  115 us
    reduce_scatter x1, waiting for transfers between devices, on_device(): lax.psum_scatter(lax.dot_general(dy_all, w_out, (((1,), (1,)), ((), ())),...  100 us
    all_gather x1, waiting for transfers between devices, on_device(): grad_pre_all = lax.all_gather(grad_pre, 'row', axis=0, tiled=True)  74.1 us
    unnamed x5, local copies, waits for them, and re-layouts  51 us
    reduce_scatter x1, waiting for transfers between devices, on_device(): lax.psum_scatter(lax.dot_general(grad_pre_all, w_in, (((1,), (1,)), ((),...  20.4 us
  transfers between devices with their start and end apart: 8, of which 8 were waited for; matrix products, arithmetic and copies ran while one was open for 14% of the time, Pallas kernels for 0%

commit v1 on v0

v1 whole, which is shorter than its diff:
```python
import jax
import jax.numpy as jnp
from jax import lax
from jax.sharding import PartitionSpec as P

gelu_c = 0.7978845608028654
gelu_k = 0.044715


def gelu_pair(preact):
    inner = gelu_c * (preact + gelu_k * preact * preact * preact)
    tangent = jnp.tanh(inner)
    gelu_value = 0.5 * preact * (1.0 + tangent)
    gelu_slope = 0.5 * (1.0 + tangent) + 0.5 * preact * (1.0 - tangent * tangent) * gelu_c * (
        1.0 + 3.0 * gelu_k * preact * preact
    )
    return (gelu_value, gelu_slope)


CHUNKS = 2


def on_device(n_depth, inputs, cotangent, w_in, w_out):
    depth = lax.axis_index("depth")
    units = w_in.shape[1] // n_depth
    x_all = lax.all_gather(inputs, ("depth", "col"), axis=0, tiled=True)
    dy_all = lax.all_gather(cotangent, ("depth", "col"), axis=0, tiled=True)
    size = units // CHUNKS
    hiddens, grad_pres, w_ins, w_outs = [], [], [], []
    slopes, h_scat, g_scat = [], [], []
    for c in range(CHUNKS):
        start = depth * units + c * size
        w_ins.append(lax.dynamic_slice_in_dim(w_in, start, size, 1))
        w_outs.append(lax.dynamic_slice_in_dim(w_out, start, size, 0))
    for c in range(CHUNKS):
        preact = lax.psum_scatter(
            jnp.dot(x_all, w_ins[c], preferred_element_type=jnp.float32).astype(jnp.bfloat16),
            "row", scatter_dimension=0, tiled=True,
        ).astype(jnp.float32)
        grad_hidden = lax.psum_scatter(
            lax.dot_general(
                dy_all, w_outs[c], (((1,), (1,)), ((), ())), preferred_element_type=jnp.float32
            ).astype(jnp.bfloat16),
            "row", scatter_dimension=0, tiled=True,
        )
        gelu_value, gelu_slope = gelu_pair(preact)
        hiddens.append(lax.all_gather(gelu_value.astype(jnp.bfloat16), "row", axis=0, tiled=True))
        grad_pre = (grad_hidden.astype(jnp.float32) * gelu_slope).astype(jnp.bfloat16)
        grad_pres.append(lax.all_gather(grad_pre, "row", axis=0, tiled=True))
    outputs = 0.0
    grad_inputs = 0.0
    g_w_in, g_w_out = [], []
    half = w_out.shape[1] // n_depth
    for c in range(CHUNKS):
        g_w_out.append(lax.dot_general(
            hiddens[c], dy_all, (((0,), (0,)), ((), ())), preferred_element_type=jnp.float32
        ).astype(jnp.bfloat16))
        outputs += jnp.dot(hiddens[c], w_outs[c], preferred_element_type=jnp.float32)
        grad_inputs += lax.dot_general(
            grad_pres[c], w_ins[c], (((1,), (1,)), ((), ())), preferred_element_type=jnp.float32
        )
        g_w_in.append(lax.dot_general(
            x_all, grad_pres[c], (((0,), (0,)), ((), ())), preferred_element_type=jnp.float32
        ).astype(jnp.bfloat16))
    outputs = lax.psum_scatter(
        outputs.astype(jnp.bfloat16), ("depth", "col"), scatter_dimension=0, tiled=True)
    grad_inputs = lax.psum_scatter(
        grad_inputs.astype(jnp.bfloat16), ("depth", "col"), scatter_dimension=0, tiled=True)
    grad_w_in = jnp.concatenate(g_w_in, axis=1)
    grad_w_out = lax.all_to_all(
        jnp.concatenate(g_w_out, axis=0), "depth", split_axis=1, concat_axis=0, tiled=True)
    return (outputs, grad_inputs, grad_w_in, grad_w_out)


def solution(mesh):
    in_specs = (
        P(("depth", "col"), "row"),
        P(("depth", "col"), "row"),
        P("row", "col"),
        P("col", "row"),
    )
    out_specs = (
        P(("depth", "col"), "row"),
        P(("depth", "col"), "row"),
        P("row", ("col", "depth")),
        P("col", ("row", "depth")),
    )

    def body(*args):
        return on_device(mesh.shape["depth"], *args)

    return jax.shard_map(
        body, mesh=mesh, in_specs=in_specs, out_specs=out_specs, check_vma=False
    )
```

time: 1010 us -> 804 us (0.80); the launches traced: 1010 us -> 794 us
  waiting for transfers between devices: 809 us -> 556 us
  other arithmetic: 4.86 us -> 35.9 us
  blocking collectives: 23.9 us -> 0 us
  local copies, waits for them, and re-layouts: 51 us -> 73.6 us
    reduce_scatter x5 -> x2, waiting for transfers between devices: 459 us -> 0.01 us  [the longest x1 0.01 us: on_device(): lax.psum_scatter(grad_inputs.astype(jnp.bfloat16), ('depth', 'col'), scat...]
    all_gather x1 -> x4, waiting for transfers between devices: 74.1 us -> 165 us  [the longest x2 116 us: on_device(): grad_pres.append(lax.all_gather(grad_pre, 'row', axis=0, tiled=True))]
    unnamed x9 -> x16, waiting for transfers between devices: 161 us -> 223 us
    all_to_all x0 -> x1, waiting for transfers between devices: none -> 57 us  [on_device(): lax.all_to_all(jnp.concatenate(g_w_out, axis=0), 'depth', split_axis=1, c...]
    concatenate x0 -> x2, other arithmetic: none -> 31.1 us  [the longest x1 15.6 us: on_device(): grad_w_in = jnp.concatenate(g_w_in, axis=1)]
    all_gather x2 -> x0, blocking collectives: 23.9 us -> none  [the longest x1 13 us: on_device(): lax.all_gather(cotangent, 'col', axis=0, tiled=True)]
    unnamed x5 -> x22, local copies, waits for them, and re-layouts: 51 us -> 65.1 us
    all_gather x1 -> x2, waiting for transfers between devices: 115 us -> 111 us  [on_device(): lax.all_gather(gelu_value.astype(jnp.bfloat16), 'row', axis=0, tiled=True)]
  transfers between devices with their start and end apart: 8 -> 13, of which waited for: 8 -> 11; matrix products, arithmetic and copies ran while one was open for 14% -> 26% of each run, Pallas kernels for 0% -> 0%
where the time goes in v1:
time: 804 us; the launch traced here: 794 us
  waiting for transfers between devices  556 us (69%)
  matrix products  106 us (13%)
  local copies, waits for them, and re-layouts  73.6 us (9%)
  other arithmetic  35.9 us (4%)
  between operations  14.6 us (2%)
  starting transfers between devices  8.17 us (1%)
    unnamed x16, waiting for transfers between devices  223 us
    all_gather x2, waiting for transfers between devices, on_device(): grad_pres.append(lax.all_gather(grad_pre, 'row', axis=0, tiled=True))  116 us
    all_gather x2, waiting for transfers between devices, on_device(): lax.all_gather(gelu_value.astype(jnp.bfloat16), 'row', axis=0, tiled=True)  111 us
    unnamed x22, local copies, waits for them, and re-layouts  65.1 us
    all_to_all x1, waiting for transfers between devices, on_device(): lax.all_to_all(jnp.concatenate(g_w_out, axis=0), 'depth', split_axis=1, c...  57 us
    all_gather x1, waiting for transfers between devices, on_device(): dy_all = lax.all_gather(cotangent, ('depth', 'col'), axis=0, tiled=True)  34.8 us
    dot_general x2, matrix products, on_device(): lax.dot_general(grad_pres[c], w_ins[c], (((1,), (1,)), ((), ())), preferr...  19.8 us
    dot_general x2, matrix products, on_device(): jnp.dot(x_all, w_ins[c], preferred_element_type=jnp.float32)  18.5 us
  transfers between devices with their start and end apart: 13, of which 11 were waited for; matrix products, arithmetic and copies ran while one was open for 26% of the time, Pallas kernels for 0%

profile of v1, /device:TPU:0, one launch (start us, length us, event | category | flops | bytes accessed | tf_op | source)
XLA Modules:
  0.0 794.4 jit_solution(4876179482934956642)
XLA Ops:
  8.7 34.8 %all-gather.13.cloned.1.call-done = bf16[1024,768]{1,0:T(8,128)(2,1)} async-done(((bf16[256,768]{1,0:T(8,128)(2,1)}), bf16[1024,768]{1,0:T(8,128)(2,1)}) %all-gather.13.cloned.1.call-update) | async-done | bytes 1572880 | tf_op jit(solution)/shard_map/all_gather | solution.py:27
  43.5 9.1 %convert_bitcast_fusion = bf16[1024,3072]{0,1:T(8,128)(2,1)} fusion(bf16[1024,768]{1,0:T(8,128)(2,1)} %all-gather.13.cloned.1.call-done, bf16[12288,768]{1,0:T(8,128)(2,1)} %param.7, s32[]{:T(128)S(6)} %select_n.9), kind=kOutput, calls=%fused_computation.3 | convolution fusion | flops 4834983936 | bytes 12582916 | tf_op jit(solution)/shard_map/dot_general | solution.py:41
  61.4 15.0 %all-gather.7.cloned.1.call-done = bf16[1024,768]{1,0:T(8,128)(2,1)} async-done(((bf16[256,768]{1,0:T(8,128)(2,1)}), bf16[1024,768]{1,0:T(8,128)(2,1)}) %all-gather.7.cloned.1.call-update) | async-done | bytes 1572880 | tf_op jit(solution)/shard_map/all_gather | solution.py:26
  76.4 9.2 %convert_bitcast_fusion.2 = bf16[1024,3072]{0,1:T(8,128)(2,1)} fusion(bf16[1024,768]{1,0:T(8,128)(2,1)} %all-gather.7.cloned.1.call-done, bf16[768,12288]{1,0:T(8,128)(2,1)} %param.6, s32[]{:T(128)S(6)} %select_n.9), kind=kOutput, calls=%fused_computation.5 | convolution fusion | flops 4834983936 | bytes 12582916 | tf_op jit(solution)/shard_map/dot_general | solution.py:37
  95.6 9.3 %convert_bitcast_fusion.1 = bf16[1024,3072]{0,1:T(8,128)(2,1)} fusion(bf16[1024,768]{1,0:T(8,128)(2,1)S(1)} %copy-done.3, bf16[12288,768]{1,0:T(8,128)(2,1)} %param.7, s32[]{:T(128)S(6)} %select_n.8), kind=kOutput, calls=%fused_computation.4 | convolution fusion | flops 4834983936 | bytes 12582916 | tf_op jit(solution)/shard_map/dot_general | solution.py:41
  114.9 9.4 %convert_bitcast_fusion.3 = bf16[1024,3072]{0,1:T(8,128)(2,1)} fusion(bf16[1024,768]{1,0:T(8,128)(2,1)S(1)} %copy-done.1, bf16[768,12288]{1,0:T(8,128)(2,1)} %param.6, s32[]{:T(128)S(6)} %select_n.8), kind=kOutput, calls=%fused_computation.6 | convolution fusion | flops 4834983936 | bytes 12582916 | tf_op jit(solution)/shard_map/dot_general | solution.py:37
  133.4 15.2 %reduce-scatter.25.cloned.1.call-done = bf16[128,3072]{1,0:T(8,128)(2,1)} async-done(((bf16[1024,3072]{1,0:T(8,128)(2,1)}), bf16[128,3072]{1,0:T(8,128)(2,1)}) %reduce-scatter.25.cloned.1.call-update) | async-done | bytes 786448
  150.0 69.4 %reduce-scatter.21.cloned.1.call-done = bf16[128,3072]{1,0:T(8,128)(2,1)} async-done(((bf16[1024,3072]{1,0:T(8,128)(2,1)}), bf16[128,3072]{1,0:T(8,128)(2,1)}) %reduce-scatter.21.cloned.1.call-update) | async-done | bytes 786448
  223.4 66.4 %reduce-scatter.23.cloned.1.call-done = bf16[128,3072]{1,0:T(8,128)(2,1)} async-done(((bf16[1024,3072]{1,0:T(8,128)(2,1)}), bf16[128,3072]{1,0:T(8,128)(2,1)}) %reduce-scatter.23.cloned.1.call-update) | async-done | bytes 786448
  291.4 68.9 %reduce-scatter.19.cloned.1.call-done = bf16[128,3072]{1,0:T(8,128)(2,1)} async-done(((bf16[1024,3072]{1,0:T(8,128)(2,1)}), bf16[128,3072]{1,0:T(8,128)(2,1)}) %reduce-scatter.19.cloned.1.call-update) | async-done | bytes 786448
  365.5 60.4 %all-gather.17.cloned.1.call-done = bf16[1024,3072]{0,1:T(8,128)(2,1)} async-done(((bf16[128,3072]{0,1:T(8,128)(2,1)}), bf16[1024,3072]{0,1:T(8,128)(2,1)}) %all-gather.17.cloned.1.call-update) | async-done | bytes 6291472 | tf_op jit(solution)/shard_map/all_gather | solution.py:49
  426.0 9.8 %fusion.5 = f32[1024,768]{1,0:T(8,128)} fusion(bf16[1024,3072]{0,1:T(8,128)(2,1)} %all-gather.17.cloned.1.call-done, bf16[768,12288]{1,0:T(8,128)(2,1)} %param.6, s32[]{:T(128)S(6)} %select_n.9), kind=kOutput, calls=%fused_computation.16 | convolution fusion | flops 4831838208 | bytes 14155780 | tf_op jit(solution)/shard_map/dot_general | solution.py:59
  435.7 55.2 %all-gather.15.cloned.1.call-done = bf16[1024,3072]{0,1:T(8,128)(2,1)} async-done(((bf16[128,3072]{0,1:T(8,128)(2,1)}), bf16[1024,3072]{0,1:T(8,128)(2,1)}) %all-gather.15.cloned.1.call-update) | async-done | bytes 6291472 | tf_op jit(solution)/shard_map/all_gather | solution.py:49
  490.9 10.0 %add_convert_fusion = bf16[1024,768]{1,0:T(8,128)(2,1)} fusion(f32[1024,768]{1,0:T(8,128)} %fusion.5, bf16[1024,3072]{0,1:T(8,128)(2,1)} %all-gather.15.cloned.1.call-done, bf16[768,12288]{1,0:T(8,128)(2,1)} %param.6, s32[]{:T(128)S(6)} %select_n.8), kind=kOutput, calls=%fused_computation.39 | convolution fusion | flops 4833411072 | bytes 15728644 | tf_op jit(solution)/shard_map/dot_general | solution.py:59
  501.0 55.5 %all-gather.11.cloned.1.call-done = bf16[1024,3072]{0,1:T(8,128)(2,1)} async-done(((bf16[128,3072]{0,1:T(8,128)(2,1)}), bf16[1024,3072]{0,1:T(8,128)(2,1)}) %all-gather.11.cloned.1.call-update) | async-done | bytes 6291472 | tf_op jit(solution)/shard_map/all_gather | solution.py:47
  556.5 9.4 %convolution_convert_fusion = bf16[3072,768]{1,0:T(8,128)(2,1)} fusion(bf16[1024,3072]{0,1:T(8,128)(2,1)} %all-gather.11.cloned.1.call-done, bf16[1024,768]{1,0:T(8,128)(2,1)S(1)} %copy-done.3), kind=kOutput, calls=%fused_computation.7 | convolution fusion | flops 4834197504 | bytes 12582912 | tf_op jit(solution)/shard_map/dot_general | solution.py:55
  565.9 55.5 %all-gather.9.cloned.1.call-done = bf16[1024,3072]{0,1:T(8,128)(2,1)} async-done(((bf16[128,3072]{0,1:T(8,128)(2,1)}), bf16[1024,3072]{0,1:T(8,128)(2,1)}) %all-gather.9.cloned.1.call-update) | async-done | bytes 6291472 | tf_op jit(solution)/shard_map/all_gather | solution.py:47
  629.7 15.5 %pad_maximum_fusion.1 = bf16[6144,768]{1,0:T(8,128)(2,1)} fusion(bf16[3072,768]{1,0:T(8,128)(2,1)S(1)} %copy-done, bf16[3072,768]{1,0:T(8,128)(2,1)S(1)} %convolution_convert_fusion.1), kind=kLoop, calls=%fused_computation.2 | loop fusion | flops 18874368 | bytes 18874368 | tf_op jit(solution)/shard_map/concatenate | solution.py:71
  661.1 8.7 %fusion.3 = f32[1024,768]{1,0:T(8,128)S(1)} fusion(bf16[1024,3072]{0,1:T(8,128)(2,1)} %all-gather.11.cloned.1.call-done, bf16[12288,768]{1,0:T(8,128)(2,1)} %param.7, s32[]{:T(128)S(6)} %select_n.9), kind=kOutput, calls=%fused_computation.14 | convolution fusion | flops 4831838208 | bytes 14155780 | tf_op jit(solution)/shard_map/dot_general | solution.py:58
  669.8 9.7 %add_convert_fusion.1 = bf16[1024,768]{1,0:T(8,128)(2,1)} fusion(f32[1024,768]{1,0:T(8,128)S(1)} %fusion.3, bf16[1024,3072]{0,1:T(8,128)(2,1)} %all-gather.9.cloned.1.call-done, bf16[12288,768]{1,0:T(8,128)(2,1)} %param.7, s32[]{:T(128)S(6)} %select_n.8), kind=kOutput, calls=%fused_computation.40 | convolution fusion | flops 4833411072 | bytes 15728644 | tf_op jit(solution)/shard_map/dot_general | solution.py:58
  692.7 15.6 %pad_maximum_fusion = bf16[768,6144]{0,1:T(8,128)(2,1)} fusion(bf16[768,3072]{0,1:T(8,128)(2,1)S(1)} %fusion.1, bf16[768,3072]{0,1:T(8,128)(2,1)S(1)} %fusion), kind=kLoop, calls=%fused_computation.1 | loop fusion | flops 18874368 | bytes 18874368 | tf_op jit(solution)/shard_map/concatenate | solution.py:69
  708.3 12.6 %copy.11 = bf16[768,6144]{1,0:T(8,128)(2,1)} copy(bf16[768,6144]{0,1:T(8,128)(2,1)} %pad_maximum_fusion) | data formatting | bytes 18874368
  720.9 57.0 %all-to-all-done = bf16[6144,2,384]{2,0,1:T(8,128)(2,1)} async-done(((bf16[6144,2,384]{2,0,1:T(8,128)(2,1)}), bf16[6144,2,384]{2,0,1:T(8,128)(2,1)}, u32[]{:S(2)}, u32[]{:S(2)}) %all-to-all-start) | async-done | bytes 9437216 | tf_op jit(solution)/shard_map/all_to_all | solution.py:70
  778.0 9.3 %copy.24 = bf16[12288,384]{1,0:T(8,128)(2,1)} copy(bf16[12288,384]{1,0:T(8,128)(2,1)} %bitcast.7) | data formatting | bytes 18874368
  (54 shorter events, 88.8 us)
Async XLA Ops:
  7.2 36.4 %all-gather.13.cloned.1.call-start = ((), (), s32[]{:S(2)}) async-start(), calls=%async_computation.11 | async-start | bytes 1966080 | tf_op jit(solution)/shard_map/all_gather | solution.py:27
  7.9 68.5 %all-gather.7.cloned.1.call-start = ((), (), s32[]{:S(2)}) async-start(), calls=%async_computation.7 | async-start | bytes 1966080 | tf_op jit(solution)/shard_map/all_gather | solution.py:26
  8.6 139.9 %reduce-scatter.25.cloned.1.call-start = ((), (), s32[]{:S(2)}) async-start(), calls=%async_computation.18 | async-start | bytes 7077888
  61.3 158.1 %reduce-scatter.21.cloned.1.call-start = ((), (), s32[]{:S(2)}) async-start(), calls=%async_computation.16 | async-start | bytes 7077888
  94.2 1.4 copy-start.3
  94.2 195.7 %reduce-scatter.23.cloned.1.call-start = ((), (), s32[]{:S(2)}) async-start(), calls=%async_computation.17 | async-start | bytes 7077888
  113.5 1.4 copy-start.1
  113.5 246.7 %reduce-scatter.19.cloned.1.call-start = ((), (), s32[]{:S(2)}) async-start(), calls=%async_computation.15 | async-start | bytes 7077888
  133.0 293.0 %all-gather.17.cloned.1.call-start = ((), (), s32[]{:S(2)}) async-start(), calls=%async_computation.13 | async-start | bytes 7077888 | tf_op jit(solution)/shard_map/all_gather | solution.py:49
  223.4 267.6 %all-gather.15.cloned.1.call-start = ((), (), s32[]{:S(2)}) async-start(), calls=%async_computation.12 | async-start | bytes 7077888 | tf_op jit(solution)/shard_map/all_gather | solution.py:49
  364.2 192.3 %all-gather.11.cloned.1.call-start = ((), (), s32[]{:S(2)}) async-start(), calls=%async_computation.9 | async-start | bytes 7077888 | tf_op jit(solution)/shard_map/all_gather | solution.py:47
  364.9 256.4 %all-gather.9.cloned.1.call-start = ((), (), s32[]{:S(2)}) async-start(), calls=%async_computation.8 | async-start | bytes 7077888 | tf_op jit(solution)/shard_map/all_gather | solution.py:47
  365.5 412.5 %reduce-scatter.17.cloned.1.call-start = ((), (), s32[]{:S(2)}) async-start(), calls=%async_computation.14 | async-start | bytes 1966080 | tf_op jit(solution)/shard_map/reduce_scatter | solution.py:67
  621.3 8.4 %copy-start = (bf16[3072,768]{1,0:T(8,128)(2,1)S(1)}, bf16[3072,768]{1,0:T(8,128)(2,1)}, u32[]{:S(2)}) copy-start(bf16[3072,768]{1,0:T(8,128)(2,1)} %convolution_convert_fusion) | copy-start | bytes 14155780
  653.7 124.3 %all-to-all-start = ((bf16[6144,2,384]{2,0,1:T(8,128)(2,1)}), bf16[6144,2,384]{2,0,1:T(8,128)(2,1)}, u32[]{:S(2)}, u32[]{:S(2)}) async-start(bf16[6144,2,384]{2,0,1:T(8,128)(2,1)} %bitcast.39), calls=%async_computation.2 | async-start | bytes 18874368 | tf_op jit(solution)/shard_map/all_to_all | solution.py:70
  661.1 116.9 %reduce-scatter.15.cloned.1.call-start = ((), (), s32[]{:S(2)}) async-start(), calls=%async_computation.10 | async-start | bytes 1966080 | tf_op jit(solution)/shard_map/reduce_scatter | solution.py:65
  669.8 17.6 %slice-start = ((s8[6291456]{0:T(1024)(128)(4,1)}), s8[2097152]{0:T(1024)(128)(4,1)S(1)}, s32[]{:S(2)}) async-start(s8[6291456]{0:T(1024)(128)(4,1)} %bitcast.41), calls=%async_computation.19 | async-start | bytes 4194304
  679.6 7.8 slice-start.1
  679.6 7.8 copy-start.2
Sparse Core Ops, SparseCore 0:
  9.8 33.6 all-gather.12
  45.4 30.9 all-gather.6
  78.7 69.7 reduce-scatter.24
  151.3 68.1 reduce-scatter.20
  221.6 68.1 reduce-scatter.22
  292.0 68.1 reduce-scatter.18
  362.4 63.5 all-gather.16
  427.5 63.3 all-gather.14
  493.1 63.3 all-gather.10
  557.9 63.3 all-gather.8
  624.9 29.1 reduce-scatter.16
  679.7 42.2 reduce-scatter.14

commit v2 on v1

v2 whole, which is shorter than its diff:
```python
import functools

import jax
import jax.numpy as jnp
from jax import lax
from jax.experimental import pallas as pl
from jax.experimental.pallas import tpu as pltpu
from jax.sharding import PartitionSpec as P

MESH = pl.DeviceIdType.MESH
BF16 = jnp.bfloat16
F32 = jnp.float32
UNITS = 256
TILE = 64

gelu_c = 0.7978845608028654
gelu_k = 0.044715


def gelu_pair(preact):
    inner = gelu_c * (preact + gelu_k * preact * preact * preact)
    tangent = jnp.tanh(inner)
    gelu_value = 0.5 * preact * (1.0 + tangent)
    gelu_slope = 0.5 * (1.0 + tangent) + 0.5 * preact * (1.0 - tangent * tangent) * gelu_c * (
        1.0 + 3.0 * gelu_k * preact * preact
    )
    return (gelu_value, gelu_slope)


def dot(a, b, ca, cb):
    return lax.dot_general(a, b, (((ca,), (cb,)), ((), ())), preferred_element_type=F32)


def kernel(
    n_row,
    x_ref, xt_ref, dy_ref, dyk_ref, dys_ref, w_in_hbm, w_out_hbm,
    sums_ref, gwi_hbm, gwo_hbm,
    w_in, w_out, acc_o, acc_g, pk, ps, pr, total, from_left, from_right, to_right, to_left,
    hg, gwi_st, gk_st, gs_st,
    w_sem, p_send, p_recv, p_free, r_send, r_recv, r_free, l_send, l_recv, l_free,
    h_send, h_recv, h_free, gwi_sem, gk_sem, gs_send, gs_recv,
):
    n_chunks, width, units = w_in.shape
    tokens = x_ref.shape[0]
    half = tokens // 2
    nz = n_row // 2
    slots = from_left.shape[0]
    row = lax.axis_index("row")
    depth = lax.axis_index("depth")
    z = row // 2
    core = row % 2
    mine = pl.multiple_of(core * half, half)
    other = pl.multiple_of((1 - core) * half, half)
    sibling = {"row": row + 1 - 2 * core}
    right = {"row": (row + 2) % n_row}
    left = {"row": (row + n_row - 2) % n_row}
    peer = {"depth": 1 - depth}
    first = depth * (n_chunks * units)

    def w_copy(c, q):
        at = pl.ds(pl.multiple_of(first + c * units, units), units)
        if q == 0:
            return pltpu.make_async_copy(w_in_hbm.at[:, at], w_in.at[c], w_sem.at[c, q])
        return pltpu.make_async_copy(w_out_hbm.at[at, :], w_out.at[c], w_sem.at[c, q])

    def remote(src, dst, send_sem, recv_sem, device):
        return pltpu.make_async_remote_copy(
            src_ref=src, dst_ref=dst, send_sem=send_sem, recv_sem=recv_sem,
            device_id=device, device_id_type=MESH,
        )

    def p_copy(c, q):
        s = c % 2
        return remote(ps.at[s, q], pr.at[s, q], p_send.at[s, q], p_recv.at[s, q], sibling)

    def r_copy(c, q):
        s, d = c % 2, c % slots
        return remote(to_right.at[s, q], from_left.at[d, q], r_send.at[s, q], r_recv.at[d, q], right)

    def l_copy(c, q):
        s, d = c % 2, c % slots
        return remote(to_left.at[s, q], from_right.at[d, q], l_send.at[s, q], l_recv.at[d, q], left)

    def h_copy(c, q):
        s = c % 2
        part = hg.at[s, q, pl.ds(mine, half), :]
        return remote(part, part, h_send.at[s, q], h_recv.at[s, q], sibling)

    def gwi_copy(c):
        at = pl.ds(pl.multiple_of(c * units, units), units)
        return pltpu.make_async_copy(gwi_st.at[c % 2], gwi_hbm.at[:, at], gwi_sem.at[c % 2])

    def gwo_rows(c):
        return gwo_hbm.at[pl.ds(pl.multiple_of(first + c * units, units), units), :]

    def gk_copy(c):
        return pltpu.make_async_copy(gk_st.at[c % 2], gwo_rows(c), gk_sem.at[c % 2])

    def gs_copy(c):
        return remote(gs_st.at[c % 2], gwo_rows(c), gs_send.at[c % 2], gs_recv.at[c], peer)

    def signal(sem, device):
        pl.semaphore_signal(sem, inc=1, device_id=device, device_id_type=MESH)

    @pl.loop(0, n_chunks)
    def _(c):
        w_copy(c, 0).start()
        w_copy(c, 1).start()

    barrier = pltpu.get_barrier_semaphore()
    signal(barrier, sibling)
    signal(barrier, peer)

    @pl.when(z > 0)
    def _():
        signal(barrier, left)

    @pl.when(z < nz - 1)
    def _():
        signal(barrier, right)

    acc_o[...] = jnp.zeros_like(acc_o)
    acc_g[...] = jnp.zeros_like(acc_g)

    @pl.when(z == 0)
    def _():
        from_left[...] = jnp.zeros_like(from_left)

    @pl.when(z == nz - 1)
    def _():
        from_right[...] = jnp.zeros_like(from_right)

    inner = jnp.logical_and(z > 0, z < nz - 1)
    pl.semaphore_wait(barrier, jnp.where(inner, 4, 3))

    def product(c, q):
        s = c % 2
        w_copy(c, q).wait()

        def part(start):
            if q == 0:
                value = dot(x_ref[pl.ds(start, half), :], w_in[c], 1, 0)
            else:
                value = dot(dy_ref[pl.ds(start, half), :], w_out[c], 1, 1)
            return value.astype(BF16)

        ps[s, q] = part(other)

        @pl.when(c >= 2)
        def _():
            pl.semaphore_wait(p_free.at[q], 1)

        p_copy(c, q).start()
        pk[s, q] = part(mine)

    def chip_sum(c, q):
        s, t = c % 2, c % nz
        p_copy(c, q).wait()

        @pl.loop(0, half, step=TILE)
        def _(i):
            at = pl.ds(pl.multiple_of(i, TILE), TILE)
            total[t, q, at, :] = pk[s, q, at, :].astype(F32) + pr[s, q, at, :].astype(F32)

        @pl.when(c < n_chunks - 2)
        def _():
            signal(p_free.at[q], sibling)

    def flow(c, q, copy, held, staged, free, has_before, has_after):
        s, t, d = c % 2, c % nz, c % slots

        @pl.when(has_before)
        def _():
            copy(c, q).wait_recv()

        @pl.when(has_after)
        def _():
            @pl.when(c >= 2)
            def _():
                copy(c, q).wait_send()

            @pl.loop(0, half, step=TILE)
            def _(i):
                at = pl.ds(pl.multiple_of(i, TILE), TILE)
                staged[s, q, at, :] = (
                    total[t, q, at, :] + held[d, q, at, :].astype(F32)
                ).astype(BF16)

            @pl.when(c >= slots)
            def _():
                pl.semaphore_wait(free.at[q], 1)

            copy(c, q).start()

    def activate(c):
        s, t, d = c % 2, c % nz, c % slots

        @pl.loop(0, half, step=TILE)
        def _(i):
            at = pl.ds(pl.multiple_of(i, TILE), TILE)
            preact, grad = (
                total[t, q, at, :]
                + from_left[d, q, at, :].astype(F32)
                + from_right[d, q, at, :].astype(F32)
                for q in range(2)
            )
            value, slope = gelu_pair(preact)
            to = pl.ds(pl.multiple_of(mine + i, TILE), TILE)
            hg[s, 0, to, :] = value.astype(BF16)
            hg[s, 1, to, :] = (grad.astype(BF16).astype(F32) * slope).astype(BF16)

        for q in range(2):

            @pl.when(jnp.logical_and(z > 0, c < n_chunks - slots))
            def _():
                signal(r_free.at[q], left)

            @pl.when(jnp.logical_and(z < nz - 1, c < n_chunks - slots))
            def _():
                signal(l_free.at[q], right)

            @pl.when(c >= 2)
            def _():
                pl.semaphore_wait(h_free.at[q], 1)

            h_copy(c, q).start()

    def rows_loop(body):
        step = min(256, tokens)

        @pl.loop(0, tokens, step=step)
        def _(i):
            body(pl.ds(pl.multiple_of(i, step), step))

    def finish(c, q):
        s = c % 2
        h_copy(c, q).wait()

        if q == 0:

            def add(at):
                acc_o[at, :] += dot(hg[s, 0, at, :], w_out[c], 1, 0)

            rows_loop(add)

            @pl.when(c >= 2)
            def _():
                gk_copy(c).wait()
                gs_copy(c).wait_send()

            gs_st[s] = dot(hg[s, 0], dys_ref[...], 0, 0).astype(BF16)
            gs_copy(c).start()
            gk_st[s] = dot(hg[s, 0], dyk_ref[...], 0, 0).astype(BF16)
            gk_copy(c).start()
        else:

            def add(at):
                acc_g[at, :] += dot(hg[s, 1, at, :], w_in[c], 1, 1)

            rows_loop(add)

            @pl.when(c >= 2)
            def _():
                gwi_copy(c).wait()

            gwi_st[s] = dot(xt_ref[...], hg[s, 1], 1, 0).astype(BF16)
            gwi_copy(c).start()

        @pl.when(c < n_chunks - 2)
        def _():
            signal(h_free.at[q], sibling)

    def at_chunk(c, body):
        @pl.when(jnp.logical_and(c >= 0, c < n_chunks))
        def _():
            body(c)

    @pl.loop(0, n_chunks + nz + 1)
    def _(step):
        for q in range(2):
            at_chunk(step - 1, lambda c: chip_sum(c, q))
            at_chunk(
                step - 1 - z,
                lambda c: flow(c, q, r_copy, from_left, to_right, r_free, z > 0, z < nz - 1),
            )
            at_chunk(
                step - nz + z,
                lambda c: flow(c, q, l_copy, from_right, to_left, l_free, z < nz - 1, z > 0),
            )
            at_chunk(step, lambda c: product(c, q))
            if q == 0:
                at_chunk(step - nz - 1, lambda c: finish(c, 0))
            else:
                at_chunk(step - nz, activate)
                at_chunk(step - nz - 1, lambda c: finish(c, 1))

    sums_ref[0] = acc_o[...].astype(BF16)
    sums_ref[1] = acc_g[...].astype(BF16)

    for c in (n_chunks - 2, n_chunks - 1):
        gwi_copy(c).wait()
        gk_copy(c).wait()
        gs_copy(c).wait_send()
        for q in range(2):

            @pl.when(z < nz - 1)
            def _():
                r_copy(c, q).wait_send()

            @pl.when(z > 0)
            def _():
                l_copy(c, q).wait_send()

    @pl.loop(0, n_chunks)
    def _(c):
        gs_copy(c).wait_recv()


def on_device(n_row, n_depth, inputs, cotangent, w_in, w_out):
    depth = lax.axis_index("depth")
    width = w_in.shape[0]
    units = w_in.shape[1] // n_depth
    both = lax.all_gather(
        jnp.stack([inputs, cotangent]), ("depth", "col"), axis=1, tiled=True
    )
    x_all, dy_all = both[0], both[1]
    tokens = x_all.shape[0]
    part = width // n_depth
    dy_keep = lax.dynamic_slice_in_dim(dy_all, depth * part, part, 1)
    dy_send = lax.dynamic_slice_in_dim(dy_all, (1 - depth) * part, part, 1)
    n_chunks = units // UNITS
    half = tokens // 2
    nz = n_row // 2
    slots = nz + 1
    dma, regular = pltpu.SemaphoreType.DMA, pltpu.SemaphoreType.REGULAR
    vmem, hbm = pl.BlockSpec(memory_space=pltpu.VMEM), pl.BlockSpec(memory_space=pl.ANY)
    sums, grad_w_in, grad_w_out = pl.pallas_call(
        functools.partial(kernel, n_row),
        out_shape=(
            jax.ShapeDtypeStruct((2, tokens, width), BF16),
            jax.ShapeDtypeStruct((width, units), BF16),
            jax.ShapeDtypeStruct((w_out.shape[0], part), BF16),
        ),
        in_specs=[vmem] * 5 + [hbm] * 2,
        out_specs=(vmem, hbm, hbm),
        scratch_shapes=[
            pltpu.VMEM((n_chunks, width, UNITS), BF16),
            pltpu.VMEM((n_chunks, UNITS, width), BF16),
            pltpu.VMEM((tokens, width), F32),
            pltpu.VMEM((tokens, width), F32),
            pltpu.VMEM((2, 2, half, UNITS), BF16),
            pltpu.VMEM((2, 2, half, UNITS), BF16),
            pltpu.VMEM((2, 2, half, UNITS), BF16),
            pltpu.VMEM((nz, 2, half, UNITS), F32),
            pltpu.VMEM((slots, 2, half, UNITS), BF16),
            pltpu.VMEM((slots, 2, half, UNITS), BF16),
            pltpu.VMEM((2, 2, half, UNITS), BF16),
            pltpu.VMEM((2, 2, half, UNITS), BF16),
            pltpu.VMEM((2, 2, tokens, UNITS), BF16),
            pltpu.VMEM((2, width, UNITS), BF16),
            pltpu.VMEM((2, UNITS, part), BF16),
            pltpu.VMEM((2, UNITS, part), BF16),
            dma((n_chunks, 2)),
            dma((2, 2)), dma((2, 2)), regular((2,)),
            dma((2, 2)), dma((slots, 2)), regular((2,)),
            dma((2, 2)), dma((slots, 2)), regular((2,)),
            dma((2, 2)), dma((2, 2)), regular((2,)),
            dma((2,)), dma((2,)), dma((2,)), dma((n_chunks,)),
        ],
        compiler_params=pltpu.CompilerParams(
            collective_id=0, has_side_effects=True, vmem_limit_bytes=60 * 1024 * 1024
        ),
        cost_estimate=pl.CostEstimate(
            flops=12 * tokens * width * units, bytes_accessed=6 * width * units * 2,
            transcendentals=tokens * units,
        ),
    )(x_all, x_all.T, dy_all, dy_keep, dy_send, w_in, w_out)
    sums = lax.psum_scatter(sums, ("depth", "col"), scatter_dimension=1, tiled=True)
    return (sums[0], sums[1], grad_w_in, grad_w_out)


def solution(mesh):
    in_specs = (
        P(("depth", "col"), "row"),
        P(("depth", "col"), "row"),
        P("row", "col"),
        P("col", "row"),
    )
    out_specs = (
        P(("depth", "col"), "row"),
        P(("depth", "col"), "row"),
        P("row", ("col", "depth")),
        P("col", ("row", "depth")),
    )
    return jax.shard_map(
        functools.partial(on_device, mesh.shape["row"], mesh.shape["depth"]),
        mesh=mesh, in_specs=in_specs, out_specs=out_specs, check_vma=False,
    )
```

time: 804 us -> 443 us (0.55); the launches traced: 794 us -> 442 us
  waiting for transfers between devices: 556 us -> 89.7 us
  Pallas kernels: 0 us -> 310 us
  matrix products: 106 us -> 0 us
  local copies, waits for them, and re-layouts: 73.6 us -> 26.9 us
  other arithmetic: 35.9 us -> 2.07 us
  starting transfers between devices: 8.17 us -> 0.08 us
    pallas_call x0 -> x1, Pallas kernels: none -> 310 us  [on_device(): pl.pallas_call(functools.partial(kernel, n_row), out_shape=(jax.ShapeDtyp...]
    all_gather x6 -> x1, waiting for transfers between devices: 276 us -> 47.8 us  [on_device(): lax.all_gather(jnp.stack([inputs, cotangent]), ('depth', 'col'), axis=1,...]
    unnamed x16 -> x2, waiting for transfers between devices: 223 us -> 0.03 us
    dot_general x12 -> x0, matrix products: 106 us -> none  [the longest x2 19.8 us: on_device(): lax.dot_general(grad_pres[c], w_ins[c], (((1,), (1,)), ((), ())), preferr...]
    all_to_all x1 -> x0, waiting for transfers between devices: 57 us -> none  [on_device(): lax.all_to_all(jnp.concatenate(g_w_out, axis=0), 'depth', split_axis=1, c...]
    unnamed x22 -> x2, local copies, waits for them, and re-layouts: 65.1 us -> 17.9 us
    reduce_scatter x2 -> x1, waiting for transfers between devices: 0.01 us -> 41.9 us  [on_device(): lax.psum_scatter(sums, ('depth', 'col'), scatter_dimension=1, tiled=True)]
    concatenate x2 -> x0, other arithmetic: 31.1 us -> none  [the longest x1 15.6 us: on_device(): grad_w_in = jnp.concatenate(g_w_in, axis=1)]
  transfers between devices with their start and end apart: 13 -> 2, of which waited for: 11 -> 2; matrix products, arithmetic and copies ran while one was open for 26% -> 0% of each run, Pallas kernels for 0% -> 0%
where the time goes in v2:
time: 443 us; the launch traced here: 442 us
  Pallas kernels  310 us (70%)
  waiting for transfers between devices  89.7 us (20%)
  local copies, waits for them, and re-layouts  26.9 us (6%)
  between operations  14.1 us (3%)
    pallas_call x1, Pallas kernels, on_device(): pl.pallas_call(functools.partial(kernel, n_row), out_shape=(jax.ShapeDtyp...  310 us
    all_gather x1, waiting for transfers between devices, on_device(): lax.all_gather(jnp.stack([inputs, cotangent]), ('depth', 'col'), axis=1,...  47.8 us
    reduce_scatter x1, waiting for transfers between devices, on_device(): lax.psum_scatter(sums, ('depth', 'col'), scatter_dimension=1, tiled=True)  41.9 us
    unnamed x2, local copies, waits for them, and re-layouts  17.9 us
  transfers between devices with their start and end apart: 2, of which 2 were waited for; matrix products, arithmetic and copies ran while one was open for 0% of the time, Pallas kernels for 0%

profile of v2, /device:TPU:0, one launch (start us, length us, event | category | flops | bytes accessed | tf_op | source)
XLA Modules:
  0.0 442.3 jit_solution(2749711161852098900)
XLA Ops:
  7.2 0.0 all-gather.2.cloned.1.call-start
  7.2 2.1 pad_maximum_fusion
  9.3 0.0 all-gather.2.cloned.1.call-update
  9.3 0.0 reduce-scatter.2.cloned.1.call-start
  9.4 47.8 %all-gather.2.cloned.1.call-done = bf16[2,1024,768]{2,1,0:T(8,128)(2,1)} async-done(((bf16[2,256,768]{2,1,0:T(8,128)(2,1)}), bf16[2,1024,768]{2,1,0:T(8,128)(2,1)}) %all-gather.2.cloned.1.call-update) | async-done | bytes 3145744 | tf_op jit(solution)/shard_map/all_gather | solution.py:323
  57.1 3.9 fusion
  61.1 1.7 copy.8.xt_ref
  62.7 1.4 dynamic-slice_bitcast_fusion
  64.1 309.5 %shard_map.75 = (bf16[2,1024,768]{2,1,0:T(8,128)(2,1)}, bf16[768,6144]{1,0:T(8,128)(2,1)}, bf16[12288,384]{1,0:T(8,128)(2,1)}) custom-call(bf16[1024,768]{1,0:T(8,128)(2,1)} %get-tuple-element.13.x_ref, bf16[768,1024]{1,0:T(8,128)(2,1)} %copy.8.xt_ref, bf16[1024,768]{1,0:T(8,128)(2,1)} %get-tuple-element.11.dy_ref, ...), custom_call_target="tpu_custom_call" | custom-call | flops 57982058496 | bytes 56623104 | tf_op jit(solution)/shard_map/pallas_call | solution.py:337
  373.7 0.0 reduce-scatter.2.cloned.1.call-update
  373.7 41.9 %reduce-scatter.2.cloned.1.call-done = bf16[2,256,768]{2,1,0:T(8,128)(2,1)} async-done(((bf16[2,1024,768]{2,1,0:T(8,128)(2,1)}), bf16[2,256,768]{2,1,0:T(8,128)(2,1)}) %reduce-scatter.2.cloned.1.call-update) | async-done | bytes 786448 | tf_op jit(solution)/shard_map/reduce_scatter | solution.py:378
  415.5 2.0 slice_bitcast_fusion.2
  417.6 8.6 %copy.11 = bf16[768,6144]{1,0:T(8,128)(2,1)} copy(bf16[768,6144]{1,0:T(8,128)(2,1)} %get-tuple-element.24) | data formatting | bytes 18874368
  426.2 9.3 %copy.12 = bf16[12288,384]{1,0:T(8,128)(2,1)} copy(bf16[12288,384]{1,0:T(8,128)(2,1)} %get-tuple-element.25) | data formatting | bytes 18874368
Async XLA Ops:
  7.2 50.0 %all-gather.2.cloned.1.call-start = ((), (), s32[]{:S(2)}) async-start(), calls=%async_computation.1 | async-start | bytes 3932160 | tf_op jit(solution)/shard_map/all_gather | solution.py:323
  9.3 406.2 %reduce-scatter.2.cloned.1.call-start = ((), (), s32[]{:S(2)}) async-start(), calls=%async_computation.2 | async-start | bytes 3932160 | tf_op jit(solution)/shard_map/reduce_scatter | solution.py:378
Sparse Core Ops, SparseCore 0:
  10.4 46.6 all-gather.1
  373.8 41.6 reduce-scatter.1

commit v3 on v2

v3 whole, which is shorter than its diff:
```python
import functools

import jax
import jax.numpy as jnp
from jax import lax
from jax.experimental import pallas as pl
from jax.experimental.pallas import tpu as pltpu
from jax.sharding import PartitionSpec as P

MESH = pl.DeviceIdType.MESH
BF16 = jnp.bfloat16
F32 = jnp.float32
UNITS = 256
TILE = 64

gelu_c = 0.7978845608028654
gelu_k = 0.044715


def gelu_pair(preact):
    inner = gelu_c * (preact + gelu_k * preact * preact * preact)
    tangent = jnp.tanh(inner)
    gelu_value = 0.5 * preact * (1.0 + tangent)
    gelu_slope = 0.5 * (1.0 + tangent) + 0.5 * preact * (1.0 - tangent * tangent) * gelu_c * (
        1.0 + 3.0 * gelu_k * preact * preact
    )
    return (gelu_value, gelu_slope)


def dot(a, b, ca, cb):
    return lax.dot_general(a, b, (((ca,), (cb,)), ((), ())), preferred_element_type=F32)


def kernel(
    n_row, n_depth, n_col,
    x_block, dy_block, w_in_hbm, w_out_hbm,
    out_ref, gin_ref, gwi_hbm, gwo_hbm,
    x_ref, xt_ref, dy_ref, dyk_ref, dys_ref, sums, parts,
    w_in, w_out, acc_o, acc_g, pk, ps, pr, total, from_left, from_right, to_right, to_left,
    hg, gwi_st, gk_st, gs_st,
    w_sem, p_send, p_recv, p_free, r_send, r_recv, r_free, l_send, l_recv, l_free,
    h_send, h_recv, h_free, gwi_sem, gk_sem, gs_send, gs_recv,
    a_send, a_recv, s_send, s_recv,
):
    n_chunks, width, units = w_in.shape
    n_sub = 2 * n_chunks
    tokens = x_ref.shape[0]
    half = tokens // 2
    quarter = half // 2
    block = x_block.shape[0]
    n_plane = n_depth * n_col
    nz = n_row // 2
    slots = from_left.shape[0]
    stages = to_right.shape[0]
    row = lax.axis_index("row")
    depth = lax.axis_index("depth")
    plane = depth * n_col + lax.axis_index("col")
    z = row // 2
    core = row % 2
    sibling = {"row": row + 1 - 2 * core}
    right = {"row": (row + 2) % n_row}
    left = {"row": (row + n_row - 2) % n_row}
    peer = {"depth": 1 - depth}
    first = depth * (n_chunks * units)

    def rows_of(u, which):
        return pl.ds(pl.multiple_of((u % 2) * half + which * quarter, quarter), quarter)

    def plane_peer(k):
        other = (plane + k) % n_plane
        return other, {"depth": other // n_col, "col": other % n_col}

    def block_rows(index):
        return pl.ds(pl.multiple_of(index * block, block), block)

    def a_copy(q, k):
        src, dst = ((x_block, x_ref), (dy_block, dy_ref))[q]
        return remote(
            src, dst.at[block_rows(plane), :], a_send.at[q, k - 1], a_recv.at[q, k - 1],
            plane_peer(k)[1],
        )

    def s_copy(q, k):
        other, device = plane_peer(k)
        return remote(
            sums.at[q, block_rows(other), :], parts.at[q, k - 1],
            s_send.at[q, k - 1], s_recv.at[q, k - 1], device,
        )

    def w_copy(c, q):
        at = pl.ds(pl.multiple_of(first + c * units, units), units)
        if q == 0:
            return pltpu.make_async_copy(w_in_hbm.at[:, at], w_in.at[c], w_sem.at[c, q])
        return pltpu.make_async_copy(w_out_hbm.at[at, :], w_out.at[c], w_sem.at[c, q])

    def remote(src, dst, send_sem, recv_sem, device):
        return pltpu.make_async_remote_copy(
            src_ref=src, dst_ref=dst, send_sem=send_sem, recv_sem=recv_sem,
            device_id=device, device_id_type=MESH,
        )

    def p_copy(c, q):
        s = c % 2
        return remote(ps.at[s, q], pr.at[s, q], p_send.at[s, q], p_recv.at[s, q], sibling)

    def r_copy(c, q):
        s, d = c % stages, c % slots
        return remote(to_right.at[s, q], from_left.at[d, q], r_send.at[s, q], r_recv.at[d, q], right)

    def l_copy(c, q):
        s, d = c % stages, c % slots
        return remote(to_left.at[s, q], from_right.at[d, q], l_send.at[s, q], l_recv.at[d, q], left)

    def h_copy(u, q):
        s, t = (u // 2) % 2, u % 2
        part = hg.at[s, q, rows_of(u, core), :]
        return remote(part, part, h_send.at[s, t, q], h_recv.at[s, t, q], sibling)

    def gwi_copy(c):
        at = pl.ds(pl.multiple_of(c * units, units), units)
        return pltpu.make_async_copy(gwi_st.at[c % 2], gwi_hbm.at[:, at], gwi_sem.at[c % 2])

    def gwo_rows(c):
        return gwo_hbm.at[pl.ds(pl.multiple_of(first + c * units, units), units), :]

    def gk_copy(c):
        return pltpu.make_async_copy(gk_st.at[c % 2], gwo_rows(c), gk_sem.at[c % 2])

    def gs_copy(c):
        return remote(gs_st.at[c % 2], gwo_rows(c), gs_send.at[c % 2], gs_recv.at[c], peer)

    def signal(sem, device):
        pl.semaphore_signal(sem, inc=1, device_id=device, device_id_type=MESH)

    @pl.loop(0, n_chunks)
    def _(c):
        w_copy(c, 0).start()
        w_copy(c, 1).start()

    barrier = pltpu.get_barrier_semaphore()
    signal(barrier, sibling)
    for k in range(1, n_plane):
        signal(barrier, plane_peer(k)[1])

    @pl.when(z > 0)
    def _():
        signal(barrier, left)

    @pl.when(z < nz - 1)
    def _():
        signal(barrier, right)

    acc_o[...] = jnp.zeros_like(acc_o)
    acc_g[...] = jnp.zeros_like(acc_g)

    @pl.when(z == 0)
    def _():
        from_left[...] = jnp.zeros_like(from_left)

    @pl.when(z == nz - 1)
    def _():
        from_right[...] = jnp.zeros_like(from_right)

    inner = jnp.logical_and(z > 0, z < nz - 1)
    pl.semaphore_wait(barrier, jnp.where(inner, n_plane + 2, n_plane + 1))

    for q in range(2):
        for k in range(1, n_plane):
            a_copy(q, k).start()
    x_ref[block_rows(plane), :] = x_block[...]
    dy_ref[block_rows(plane), :] = dy_block[...]

    def gathered(q):
        for k in range(1, n_plane):
            a_copy(q, k).wait()

    def arrange():
        part = width // 2
        for d in range(2):

            @pl.when(depth == d)
            def _():
                dyk_ref[...] = dy_ref[:, d * part:(d + 1) * part]
                dys_ref[...] = dy_ref[:, (1 - d) * part:(2 - d) * part]

        for i in range(0, tokens, half // 2):
            xt_ref[:, i:i + half // 2] = x_ref[i:i + half // 2, :].T

    def product(u, q):
        s, c = u % 2, u // 2

        @pl.when(u == 0)
        def _():
            gathered(q)

        @pl.when(u % 2 == 0)
        def _():
            w_copy(c, q).wait()

        def part(which):
            if q == 0:
                value = dot(x_ref[rows_of(u, which), :], w_in[c], 1, 0)
            else:
                value = dot(dy_ref[rows_of(u, which), :], w_out[c], 1, 1)
            return value.astype(BF16)

        ps[s, q] = part(1 - core)

        @pl.when(u >= 2)
        def _():
            pl.semaphore_wait(p_free.at[q], 1)

        p_copy(u, q).start()
        pk[s, q] = part(core)

    def chip_sum(c, q):
        s, t = c % 2, c % nz
        p_copy(c, q).wait()

        @pl.loop(0, quarter, step=TILE)
        def _(i):
            at = pl.ds(pl.multiple_of(i, TILE), TILE)
            total[t, q, at, :] = pk[s, q, at, :].astype(F32) + pr[s, q, at, :].astype(F32)

        @pl.when(c < n_sub - 2)
        def _():
            signal(p_free.at[q], sibling)

    def flow(c, q, copy, held, staged, free, has_before, has_after):
        s, t, d = c % stages, c % nz, c % slots

        @pl.when(has_before)
        def _():
            copy(c, q).wait_recv()

        @pl.when(has_after)
        def _():
            @pl.when(c >= stages)
            def _():
                copy(c, q).wait_send()

            @pl.loop(0, quarter, step=TILE)
            def _(i):
                at = pl.ds(pl.multiple_of(i, TILE), TILE)
                staged[s, q, at, :] = (
                    total[t, q, at, :] + held[d, q, at, :].astype(F32)
                ).astype(BF16)

            @pl.when(c >= slots)
            def _():
                pl.semaphore_wait(free.at[q], 1)

            copy(c, q).start()

    def activate(c):
        s, t, d = (c // 2) % 2, c % nz, c % slots
        mine = (c % 2) * half + core * quarter

        @pl.loop(0, quarter, step=TILE)
        def _(i):
            at = pl.ds(pl.multiple_of(i, TILE), TILE)
            preact, grad = (
                total[t, q, at, :]
                + from_left[d, q, at, :].astype(F32)
                + from_right[d, q, at, :].astype(F32)
                for q in range(2)
            )
            value, slope = gelu_pair(preact)
            to = pl.ds(pl.multiple_of(mine + i, TILE), TILE)
            hg[s, 0, to, :] = value.astype(BF16)
            hg[s, 1, to, :] = (grad.astype(BF16).astype(F32) * slope).astype(BF16)

        for q in range(2):

            @pl.when(jnp.logical_and(z > 0, c < n_sub - slots))
            def _():
                signal(r_free.at[q], left)

            @pl.when(jnp.logical_and(z < nz - 1, c < n_sub - slots))
            def _():
                signal(l_free.at[q], right)

            @pl.when(jnp.logical_and(c >= 4, c % 2 == 0))
            def _():
                pl.semaphore_wait(h_free.at[q], 1)

            h_copy(c, q).start()

    def rows_loop(body):
        step = min(256, tokens)

        @pl.loop(0, tokens, step=step)
        def _(i):
            body(pl.ds(pl.multiple_of(i, step), step))

    def finish(c, q):
        s = c % 2
        h_copy(2 * c, q).wait()
        h_copy(2 * c + 1, q).wait()

        if q == 0:

            def add(at):
                acc_o[at, :] += dot(hg[s, 0, at, :], w_out[c], 1, 0)

            rows_loop(add)

            @pl.when(c >= 2)
            def _():
                gk_copy(c).wait()
                gs_copy(c).wait_send()

            gs_st[s] = dot(hg[s, 0], dys_ref[...], 0, 0).astype(BF16)
            gs_copy(c).start()
            gk_st[s] = dot(hg[s, 0], dyk_ref[...], 0, 0).astype(BF16)
            gk_copy(c).start()
        else:

            def add(at):
                acc_g[at, :] += dot(hg[s, 1, at, :], w_in[c], 1, 1)

            rows_loop(add)

            @pl.when(c >= 2)
            def _():
                gwi_copy(c).wait()

            gwi_st[s] = dot(xt_ref[...], hg[s, 1], 1, 0).astype(BF16)
            gwi_copy(c).start()

        @pl.when(c < n_chunks - 2)
        def _():
            signal(h_free.at[q], sibling)

    def at_sub(u, body):
        @pl.when(jnp.logical_and(u >= 0, u < n_sub))
        def _():
            body(u)

    @pl.loop(0, n_sub + nz + 2)
    def _(step):
        for q in range(2):
            at_sub(step - 1, lambda u: chip_sum(u, q))
            at_sub(
                step - 1 - z,
                lambda u: flow(u, q, r_copy, from_left, to_right, r_free, z > 0, z < nz - 1),
            )
            at_sub(
                step - nz + z,
                lambda u: flow(u, q, l_copy, from_right, to_left, l_free, z < nz - 1, z > 0),
            )
            at_sub(step, lambda u: product(u, q))
            if q == 1:
                at_sub(step - nz, activate)

        @pl.when(step == 1)
        def _():
            arrange()

        def last_products(u):
            for q in range(2):

                @pl.when(u % 2 == q)
                def _():
                    finish(u // 2, q)

        at_sub(step - nz - 2, last_products)

    for q, acc in enumerate((acc_o, acc_g)):
        sums[q] = acc[...].astype(BF16)
        for k in range(1, n_plane):
            s_copy(q, k).start()

    for c in (n_chunks - 2, n_chunks - 1):
        gwi_copy(c).wait()
        gk_copy(c).wait()
        gs_copy(c).wait_send()

    for u in range(n_sub - stages, n_sub):
        for q in range(2):

            @pl.when(z < nz - 1)
            def _():
                r_copy(u, q).wait_send()

            @pl.when(z > 0)
            def _():
                l_copy(u, q).wait_send()

    for q, ref in enumerate((out_ref, gin_ref)):
        for k in range(1, n_plane):
            s_copy(q, k).wait()
        value = sums[q, block_rows(plane), :].astype(F32)
        for k in range(1, n_plane):
            value += parts[q, k - 1].astype(F32)
        ref[...] = value.astype(BF16)

    @pl.loop(0, n_chunks)
    def _(c):
        gs_copy(c).wait_recv()


def copy_kernel(a_ref, b_ref, a_out, b_out):
    a_out[...] = a_ref[...]
    b_out[...] = b_ref[...]


def copied(a, b, steps=8):
    specs = [pl.BlockSpec((v.shape[0] // steps, v.shape[1]), lambda i: (i, 0)) for v in (a, b)]
    return pl.pallas_call(
        copy_kernel, grid=(steps,), in_specs=specs, out_specs=specs,
        out_shape=[jax.ShapeDtypeStruct(v.shape, v.dtype) for v in (a, b)],
        compiler_params=pltpu.CompilerParams(vmem_limit_bytes=60 * 1024 * 1024),
    )(a, b)


def on_device(n_row, n_depth, n_col, inputs, cotangent, w_in, w_out):
    width = w_in.shape[0]
    units = w_in.shape[1] // n_depth
    block = inputs.shape[0]
    n_plane = n_depth * n_col
    tokens = block * n_plane
    part = width // n_depth
    n_chunks = units // UNITS
    quarter = tokens // 4
    nz = n_row // 2
    slots, stages = nz + 3, 3
    dma, regular = pltpu.SemaphoreType.DMA, pltpu.SemaphoreType.REGULAR
    vmem, hbm = pl.BlockSpec(memory_space=pltpu.VMEM), pl.BlockSpec(memory_space=pl.ANY)
    outputs, grad_inputs, grad_w_in, grad_w_out = pl.pallas_call(
        functools.partial(kernel, n_row, n_depth, n_col),
        out_shape=(
            jax.ShapeDtypeStruct((block, width), BF16),
            jax.ShapeDtypeStruct((block, width), BF16),
            jax.ShapeDtypeStruct((width, units), BF16),
            jax.ShapeDtypeStruct((w_out.shape[0], part), BF16),
        ),
        in_specs=[vmem] * 2 + [hbm] * 2,
        out_specs=(vmem, vmem, hbm, hbm),
        scratch_shapes=[
            pltpu.VMEM((tokens, width), BF16),
            pltpu.VMEM((width, tokens), BF16),
            pltpu.VMEM((tokens, width), BF16),
            pltpu.VMEM((tokens, part), BF16),
            pltpu.VMEM((tokens, part), BF16),
            pltpu.VMEM((2, tokens, width), BF16),
            pltpu.VMEM((2, n_plane - 1, block, width), BF16),
            pltpu.VMEM((n_chunks, width, UNITS), BF16),
            pltpu.VMEM((n_chunks, UNITS, width), BF16),
            pltpu.VMEM((tokens, width), F32),
            pltpu.VMEM((tokens, width), F32),
            pltpu.VMEM((2, 2, quarter, UNITS), BF16),
            pltpu.VMEM((2, 2, quarter, UNITS), BF16),
            pltpu.VMEM((2, 2, quarter, UNITS), BF16),
            pltpu.VMEM((nz, 2, quarter, UNITS), F32),
            pltpu.VMEM((slots, 2, quarter, UNITS), BF16),
            pltpu.VMEM((slots, 2, quarter, UNITS), BF16),
            pltpu.VMEM((stages, 2, quarter, UNITS), BF16),
            pltpu.VMEM((stages, 2, quarter, UNITS), BF16),
            pltpu.VMEM((2, 2, tokens, UNITS), BF16),
            pltpu.VMEM((2, width, UNITS), BF16),
            pltpu.VMEM((2, UNITS, part), BF16),
            pltpu.VMEM((2, UNITS, part), BF16),
            dma((n_chunks, 2)),
            dma((2, 2)), dma((2, 2)), regular((2,)),
            dma((stages, 2)), dma((slots, 2)), regular((2,)),
            dma((stages, 2)), dma((slots, 2)), regular((2,)),
            dma((2, 2, 2)), dma((2, 2, 2)), regular((2,)),
            dma((2,)), dma((2,)), dma((2,)), dma((n_chunks,)),
            dma((2, n_plane - 1)), dma((2, n_plane - 1)), dma((2, n_plane - 1)), dma((2, n_plane - 1)),
        ],
        compiler_params=pltpu.CompilerParams(
            collective_id=0, has_side_effects=True, vmem_limit_bytes=60 * 1024 * 1024
        ),
        cost_estimate=pl.CostEstimate(
            flops=12 * tokens * width * units, bytes_accessed=6 * width * units * 2,
            transcendentals=tokens * units,
        ),
    )(inputs, cotangent, w_in, w_out)
    grad_w_in, grad_w_out = copied(grad_w_in, grad_w_out)
    return (outputs, grad_inputs, grad_w_in, grad_w_out)


def solution(mesh):
    in_specs = (
        P(("depth", "col"), "row"),
        P(("depth", "col"), "row"),
        P("row", "col"),
        P("col", "row"),
    )
    out_specs = (
        P(("depth", "col"), "row"),
        P(("depth", "col"), "row"),
        P("row", ("col", "depth")),
        P("col", ("row", "depth")),
    )
    return jax.shard_map(
        functools.partial(on_device, *(mesh.shape[a] for a in ("row", "depth", "col"))),
        mesh=mesh, in_specs=in_specs, out_specs=out_specs, check_vma=False,
    )
```

time: 443 us -> 388 us (0.88)
  waiting for transfers between devices: 89.7 us -> 0 us
  Pallas kernels: 310 us -> 386 us
  local copies, waits for them, and re-layouts: 26.9 us -> 1.5 us
  between operations: 14.1 us -> 0.66 us
    pallas_call x1 -> x2, Pallas kernels: 310 us -> 386 us  [the longest x1 371 us: on_device(): pl.pallas_call(functools.partial(kernel, n_row, n_depth, n_col), out_shap...]
    all_gather x1 -> x0, waiting for transfers between devices: 47.8 us -> none  [on_device(): lax.all_gather(jnp.stack([inputs, cotangent]), ('depth', 'col'), axis=1,...]
    reduce_scatter x1 -> x0, waiting for transfers between devices: 41.9 us -> none  [on_device(): lax.psum_scatter(sums, ('depth', 'col'), scatter_dimension=1, tiled=True)]
    unnamed x2 -> x6, local copies, waits for them, and re-layouts: 17.9 us -> 1.5 us
  transfers between devices with their start and end apart: 2 -> 0, of which waited for: 2 -> 0; matrix products, arithmetic and copies ran while one was open for 0% -> 0% of each run, Pallas kernels for 0% -> 0%
where the time goes in v3:
time: 388 us
  Pallas kernels  386 us (99%)
    pallas_call x1, Pallas kernels, on_device(): pl.pallas_call(functools.partial(kernel, n_row, n_depth, n_col), out_shap...  371 us
    pallas_call x1, Pallas kernels, copied(): pl.pallas_call(copy_kernel, grid=(steps,), in_specs=specs, out_specs=spec...  15 us

profile of v3, /device:TPU:0, one launch (start us, length us, event | category | flops | bytes accessed | tf_op | source)
XLA Modules:
  0.0 387.9 jit_solution(17763087421568455478)
XLA Ops:
  0.6 370.8 %shard_map.75 = (bf16[256,768]{1,0:T(8,128)(2,1)}, bf16[256,768]{1,0:T(8,128)(2,1)}, bf16[768,6144]{1,0:T(8,128)(2,1)}, bf16[12288,384]{1,0:T(8,128)(2,1)}) custom-call(bf16[256,768]{1,0:T(8,128)(2,1)} %x_block.1, bf16[256,768]{1,0:T(8,128)(2,1)} %dy_block.1, bf16[768,12288]{1,0:T(8,128)(2,1)} %w_in_hbm.1, bf16[12288,768]{1,0:T(8,128)(2,1)} %w_out_hbm.1), custom_call_target="tpu_custom_call" | custom-call | flops 57982058496 | bytes 56623104 | tf_op jit(solution)/shard_map/pallas_call | solution.py:430
  371.4 0.0 copy-start.1
  371.4 0.0 copy-start
  371.4 15.0 %shard_map.76 = (bf16[768,6144]{1,0:T(8,128)(2,1)}, bf16[12288,384]{1,0:T(8,128)(2,1)}) custom-call(bf16[768,6144]{1,0:T(8,128)(2,1)} %get-tuple-element.12.a_ref, bf16[12288,384]{1,0:T(8,128)(2,1)} %get-tuple-element.13.b_ref), custom_call_target="tpu_custom_call" | custom-call | tf_op jit(solution)/shard_map/pallas_call | solution.py:410
  386.4 0.0 copy-done.1
  386.4 0.7 copy.10
  387.2 0.0 copy-done
  387.2 0.7 copy.11
Async XLA Ops:
  371.4 15.0 %copy-start.1 = (bf16[256,768]{1,0:T(8,128)(2,1)S(1)}, bf16[256,768]{1,0:T(8,128)(2,1)}, u32[]{:S(2)}) copy-start(bf16[256,768]{1,0:T(8,128)(2,1)} %get-tuple-element.20) | copy-start | bytes 1179652
  371.4 15.7 %copy-start = (bf16[256,768]{1,0:T(8,128)(2,1)S(1)}, bf16[256,768]{1,0:T(8,128)(2,1)}, u32[]{:S(2)}) copy-start(bf16[256,768]{1,0:T(8,128)(2,1)} %get-tuple-element.21) | copy-start | bytes 1179652

commit v4 on v3

--- a/solution.py
+++ b/solution.py
@@ -11,7 +11,7 @@
 BF16 = jnp.bfloat16
 F32 = jnp.float32
 UNITS = 256
-TILE = 64
+TILE = 128
 
 gelu_c = 0.7978845608028654
 gelu_k = 0.044715
@@ -35,8 +35,8 @@
     n_row, n_depth, n_col,
     x_block, dy_block, w_in_hbm, w_out_hbm,
     out_ref, gin_ref, gwi_hbm, gwo_hbm,
-    x_ref, xt_ref, dy_ref, dyk_ref, dys_ref, sums, parts,
-    w_in, w_out, acc_o, acc_g, pk, ps, pr, total, from_left, from_right, to_right, to_left,
+    x_ref, xt_ref, dy_ref, dyo_ref, sums, parts,
+    w_in, w_out, acc_o, acc_g, ps, pr, total, from_left, from_right, to_right, to_left,
     hg, gwi_st, gk_st, gs_st,
     w_sem, p_send, p_recv, p_free, r_send, r_recv, r_free, l_send, l_recv, l_free,
     h_send, h_recv, h_free, gwi_sem, gk_sem, gs_send, gs_recv,
@@ -54,7 +54,8 @@
     stages = to_right.shape[0]
     row = lax.axis_index("row")
     depth = lax.axis_index("depth")
-    plane = depth * n_col + lax.axis_index("col")
+    col = lax.axis_index("col")
+    plane = depth * n_col + col
     z = row // 2
     core = row % 2
     sibling = {"row": row + 1 - 2 * core}
@@ -63,12 +64,15 @@
     peer = {"depth": 1 - depth}
     first = depth * (n_chunks * units)
 
+    def first_row(u):
+        return ((u + depth) % 2) * half
+
     def rows_of(u, which):
-        return pl.ds(pl.multiple_of((u % 2) * half + which * quarter, quarter), quarter)
+        return pl.ds(pl.multiple_of(first_row(u) + which * quarter, quarter), quarter)
 
     def plane_peer(k):
-        other = (plane + k) % n_plane
-        return other, {"depth": other // n_col, "col": other % n_col}
+        d, c = (depth + k // n_col) % n_depth, (col + k % n_col) % n_col
+        return d * n_col + c, {"depth": d, "col": c}
 
     def block_rows(index):
         return pl.ds(pl.multiple_of(index * block, block), block)
@@ -101,7 +105,7 @@
 
     def p_copy(c, q):
         s = c % 2
-        return remote(ps.at[s, q], pr.at[s, q], p_send.at[s, q], p_recv.at[s, q], sibling)
+        return remote(ps.at[s, q, 1 - core], pr.at[s, q], p_send.at[s, q], p_recv.at[s, q], sibling)
 
     def r_copy(c, q):
         s, d = c % stages, c % slots
@@ -164,14 +168,15 @@
     inner = jnp.logical_and(z > 0, z < nz - 1)
     pl.semaphore_wait(barrier, jnp.where(inner, n_plane + 2, n_plane + 1))
 
-    for q in range(2):
-        for k in range(1, n_plane):
-            a_copy(q, k).start()
+    for ks in (range(1, n_col + 1), range(n_col + 1, n_plane)):
+        for q in range(2):
+            for k in ks:
+                a_copy(q, k).start()
     x_ref[block_rows(plane), :] = x_block[...]
     dy_ref[block_rows(plane), :] = dy_block[...]
 
-    def gathered(q):
-        for k in range(1, n_plane):
+    def gathered(q, t):
+        for k in range(1, n_col) if t == 0 else range(n_col, n_plane):
             a_copy(q, k).wait()
 
     def arrange():
@@ -180,8 +185,8 @@
 
             @pl.when(depth == d)
             def _():
-                dyk_ref[...] = dy_ref[:, d * part:(d + 1) * part]
-                dys_ref[...] = dy_ref[:, (1 - d) * part:(2 - d) * part]
+                dyo_ref[:, :part] = dy_ref[:, d * part:(d + 1) * part]
+                dyo_ref[:, part:] = dy_ref[:, (1 - d) * part:(2 - d) * part]
 
         for i in range(0, tokens, half // 2):
             xt_ref[:, i:i + half // 2] = x_ref[i:i + half // 2, :].T
@@ -189,38 +194,36 @@
     def product(u, q):
         s, c = u % 2, u // 2
 
-        @pl.when(u == 0)
-        def _():
-            gathered(q)
+        for t in range(2):
+
+            @pl.when(u == t)
+            def _():
+                gathered(q, t)
 
         @pl.when(u % 2 == 0)
         def _():
             w_copy(c, q).wait()
 
-        def part(which):
-            if q == 0:
-                value = dot(x_ref[rows_of(u, which), :], w_in[c], 1, 0)
-            else:
-                value = dot(dy_ref[rows_of(u, which), :], w_out[c], 1, 1)
-            return value.astype(BF16)
-
-        ps[s, q] = part(1 - core)
+        rows = pl.ds(pl.multiple_of(first_row(u), half), half)
+        if q == 0:
+            value = dot(x_ref[rows, :], w_in[c], 1, 0)
+        else:
+            value = dot(dy_ref[rows, :], w_out[c], 1, 1)
+        ps[s, q] = value.astype(BF16).reshape(2, quarter, units)
 
         @pl.when(u >= 2)
         def _():
             pl.semaphore_wait(p_free.at[q], 1)
 
         p_copy(u, q).start()
-        pk[s, q] = part(core)
 
     def chip_sum(c, q):
         s, t = c % 2, c % nz
         p_copy(c, q).wait()
 
-        @pl.loop(0, quarter, step=TILE)
-        def _(i):
-            at = pl.ds(pl.multiple_of(i, TILE), TILE)
-            total[t, q, at, :] = pk[s, q, at, :].astype(F32) + pr[s, q, at, :].astype(F32)
+        for i in range(0, quarter, TILE):
+            at = pl.ds(i, TILE)
+            total[t, q, at, :] = ps[s, q, core, at, :].astype(F32) + pr[s, q, at, :].astype(F32)
 
         @pl.when(c < n_sub - 2)
         def _():
@@ -239,9 +242,8 @@
             def _():
                 copy(c, q).wait_send()
 
-            @pl.loop(0, quarter, step=TILE)
-            def _(i):
-                at = pl.ds(pl.multiple_of(i, TILE), TILE)
+            for i in range(0, quarter, TILE):
+                at = pl.ds(i, TILE)
                 staged[s, q, at, :] = (
                     total[t, q, at, :] + held[d, q, at, :].astype(F32)
                 ).astype(BF16)
@@ -254,7 +256,7 @@
 
     def activate(c):
         s, t, d = (c // 2) % 2, c % nz, c % slots
-        mine = (c % 2) * half + core * quarter
+        mine = first_row(c) + core * quarter
 
         @pl.loop(0, quarter, step=TILE)
         def _(i):
@@ -287,7 +289,7 @@
             h_copy(c, q).start()
 
     def rows_loop(body):
-        step = min(256, tokens)
+        step = min(512, tokens)
 
         @pl.loop(0, tokens, step=step)
         def _(i):
@@ -310,9 +312,10 @@
                 gk_copy(c).wait()
                 gs_copy(c).wait_send()
 
-            gs_st[s] = dot(hg[s, 0], dys_ref[...], 0, 0).astype(BF16)
+            value = dot(hg[s, 0], dyo_ref[...], 0, 0).astype(BF16)
+            gs_st[s] = value[:, width // 2:]
             gs_copy(c).start()
-            gk_st[s] = dot(hg[s, 0], dyk_ref[...], 0, 0).astype(BF16)
+            gk_st[s] = value[:, :width // 2]
             gk_copy(c).start()
         else:
 
@@ -353,7 +356,7 @@
             if q == 1:
                 at_sub(step - nz, activate)
 
-        @pl.when(step == 1)
+        @pl.when(step == 2)
         def _():
             arrange()
 
@@ -364,12 +367,13 @@
                 def _():
                     finish(u // 2, q)
 
+                @pl.when(u == n_sub - 2 + q)
+                def _():
+                    sums[q] = (acc_o, acc_g)[q][...].astype(BF16)
+                    for k in range(1, n_plane):
+                        s_copy(q, k).start()
+
         at_sub(step - nz - 2, last_products)
-
-    for q, acc in enumerate((acc_o, acc_g)):
-        sums[q] = acc[...].astype(BF16)
-        for k in range(1, n_plane):
-            s_copy(q, k).start()
 
     for c in (n_chunks - 2, n_chunks - 1):
         gwi_copy(c).wait()
@@ -441,16 +445,14 @@
             pltpu.VMEM((tokens, width), BF16),
             pltpu.VMEM((width, tokens), BF16),
             pltpu.VMEM((tokens, width), BF16),
-            pltpu.VMEM((tokens, part), BF16),
-            pltpu.VMEM((tokens, part), BF16),
+            pltpu.VMEM((tokens, width), BF16),
             pltpu.VMEM((2, tokens, width), BF16),
             pltpu.VMEM((2, n_plane - 1, block, width), BF16),
             pltpu.VMEM((n_chunks, width, UNITS), BF16),
             pltpu.VMEM((n_chunks, UNITS, width), BF16),
             pltpu.VMEM((tokens, width), F32),
             pltpu.VMEM((tokens, width), F32),
-            pltpu.VMEM((2, 2, quarter, UNITS), BF16),
-            pltpu.VMEM((2, 2, quarter, UNITS), BF16),
+            pltpu.VMEM((2, 2, 2, quarter, UNITS), BF16),
             pltpu.VMEM((2, 2, quarter, UNITS), BF16),
             pltpu.VMEM((nz, 2, quarter, UNITS), F32),
             pltpu.VMEM((slots, 2, quarter, UNITS), BF16),

time: 388 us -> 381 us (0.982)
  Pallas kernels: 386 us -> 379 us
    pallas_call x1, Pallas kernels: 371 us -> 364 us  [on_device(): pl.pallas_call(functools.partial(kernel, n_row, n_depth, n_col), out_shap...]
where the time goes in v4:
time: 381 us
  Pallas kernels  379 us (99%)
    pallas_call x1, Pallas kernels, on_device(): pl.pallas_call(functools.partial(kernel, n_row, n_depth, n_col), out_shap...  364 us
    pallas_call x1, Pallas kernels, copied(): pl.pallas_call(copy_kernel, grid=(steps,), in_specs=specs, out_specs=spec...  15 us

profile of v4, /device:TPU:0, one launch (start us, length us, event | category | flops | bytes accessed | tf_op | source)
XLA Modules:
  0.0 380.7 jit_solution(12762269117475677032)
XLA Ops:
  0.6 363.6 %shard_map.75 = (bf16[256,768]{1,0:T(8,128)(2,1)}, bf16[256,768]{1,0:T(8,128)(2,1)}, bf16[768,6144]{1,0:T(8,128)(2,1)}, bf16[12288,384]{1,0:T(8,128)(2,1)}) custom-call(bf16[256,768]{1,0:T(8,128)(2,1)} %x_block.1, bf16[256,768]{1,0:T(8,128)(2,1)} %dy_block.1, bf16[768,12288]{1,0:T(8,128)(2,1)} %w_in_hbm.1, bf16[12288,768]{1,0:T(8,128)(2,1)} %w_out_hbm.1), custom_call_target="tpu_custom_call" | custom-call | flops 57982058496 | bytes 56623104 | tf_op jit(solution)/shard_map/pallas_call | solution.py:434
  364.2 0.0 copy-start.1
  364.3 0.0 copy-start
  364.3 15.0 %shard_map.76 = (bf16[768,6144]{1,0:T(8,128)(2,1)}, bf16[12288,384]{1,0:T(8,128)(2,1)}) custom-call(bf16[768,6144]{1,0:T(8,128)(2,1)} %get-tuple-element.12.a_ref, bf16[12288,384]{1,0:T(8,128)(2,1)} %get-tuple-element.13.b_ref), custom_call_target="tpu_custom_call" | custom-call | tf_op jit(solution)/shard_map/pallas_call | solution.py:414
  379.2 0.0 copy-done.1
  379.2 0.7 copy.10
  380.0 0.0 copy-done
  380.0 0.7 copy.11
Async XLA Ops:
  364.2 15.0 %copy-start.1 = (bf16[256,768]{1,0:T(8,128)(2,1)S(1)}, bf16[256,768]{1,0:T(8,128)(2,1)}, u32[]{:S(2)}) copy-start(bf16[256,768]{1,0:T(8,128)(2,1)} %get-tuple-element.20) | copy-start | bytes 1179652
  364.3 15.7 %copy-start = (bf16[256,768]{1,0:T(8,128)(2,1)S(1)}, bf16[256,768]{1,0:T(8,128)(2,1)}, u32[]{:S(2)}) copy-start(bf16[256,768]{1,0:T(8,128)(2,1)} %get-tuple-element.21) | copy-start | bytes 1179652
